TPU v7x, 32 devices: a whole 2x2x4 slice. The times are simulated.
32 devices in a mesh: groups: 2 (over y), elem: 4 (over z), energy: 2 (over x), rhs: 2 (over core).
Axes of the slice: x: 2, y: 2, z: 4, core: 2. Of those that a mesh axis runs over, the one named last changes fastest.
Arguments:
- ham_noise: float32 [8, 256, 256], P(('groups', 'elem')), parts along dimension 0, may hold values from -0.01171875 to 0.01171875
- channel_levels: float32 [8, 256], P(('groups', 'elem')), parts along dimension 0, may hold values from 0.2 to 1.2
- coupling_noise: float32 [8, 256, 256], P(('groups', 'elem')), parts along dimension 0, may hold values from -0.01171875 to 0.01171875
- corr_weight: float32 [8], P(('groups', 'elem')), parts along dimension 0, may hold values from 0.25 to 1
- corr_basis: float32 [512, 256], P('groups'), parts along dimension 0, may hold values from -0.1875 to 0.1875
- projector: float32 [8, 256, 256], P(('groups', 'elem')), parts along dimension 0, may hold values from -0.1875 to 0.1875
- energy_shift: float32 [4], P(('groups', 'energy')), parts along dimension 0, may hold values from 0.1 to 0.4
- sources: float32 [4, 4, 256, 256], P(('groups', 'energy'), 'elem', None, 'rhs'), parts along dimension 0, may hold values from -6 to 6
- target: float32 [4, 256, 256], P(('groups', 'energy'), None, 'rhs'), parts along dimension 0, may hold values from -6 to 6
- open_channels: int32 [4], P(('groups', 'energy')), parts along dimension 0, may hold values from 64 to 256
Outputs:
- wave_functions: float32 [4, 4, 256, 256], P(('groups', 'energy'), 'elem', None, 'rhs'), parts along dimension 0
- adjoints: float32 [4, 4, 256, 256], P(('groups', 'energy'), 'elem', None, 'rhs'), parts along dimension 0
- k_matrices: float32 [4, 256, 256], P(('groups', 'energy'), 'elem', 'rhs'), parts along dimension 0
- basis_grad: float32 [512, 256], P('groups'), parts along dimension 0
There are 2 independent parts, one for each index of `groups`. A program takes and returns all parts, laid end to end along the dimension named above; each array names one. Nothing has to cross between parts.
All inputs are finite; a program needn't handle non-finite values.
Results may differ from a plain program's by a relative error of at most 0.0003.
Values sent between devices are 32-bit elements; how exact they have to be, the bound alone decides.
No kernel may reach another device: no remote copies, remote signals or barrier semaphores. Data moves between devices by JAX's collectives and lax.ppermute only.
A program may use at most 64 MiB of HBM per device.

v0:
```python
import jax
import jax.numpy as jnp
from jax import lax
from jax.sharding import PartitionSpec as P

FULL_PRECISION = lax.Precision.HIGHEST
PENALTY = 0.5


def from_behind(value, axis, steps):
    count = lax.axis_size(axis)
    first, last = (max(0, -steps), min(count, count - steps))
    return lax.ppermute(value, axis, [(source, source + steps) for source in range(first, last)])


def chol_apply(factor, values):
    halfway = lax.linalg.triangular_solve(factor, values, left_side=True, lower=True)
    return lax.linalg.triangular_solve(
        factor, halfway, left_side=True, lower=True, transpose_a=True
    )


def matmul(lhs_block, rhs_block):
    return jnp.einsum(
        "eij,ejk->eik",
        lhs_block,
        rhs_block,
        precision=FULL_PRECISION,
        preferred_element_type=jnp.float32,
    )


def eliminate(diagonal, lower_block, upper_block, source):
    element_count = lax.axis_size("elem")
    channels = diagonal.shape[-1]
    stored = []
    stride = 1
    while stride < element_count:
        factor = jnp.linalg.cholesky(diagonal)
        solved = chol_apply(factor, jnp.concatenate([lower_block, upper_block, source], axis=2))
        from_below = from_behind(solved, "elem", stride)
        from_above = from_behind(solved, "elem", -stride)
        next_diagonal = (
            diagonal
            - matmul(lower_block, from_below[:, :, channels : 2 * channels])
            - matmul(upper_block, from_above[:, :, :channels])
        )
        next_lower = -matmul(lower_block, from_below[:, :, :channels])
        next_upper = -matmul(upper_block, from_above[:, :, channels : 2 * channels])
        next_source = (
            source
            - matmul(lower_block, from_below[:, :, 2 * channels :])
            - matmul(upper_block, from_above[:, :, 2 * channels :])
        )
        stored.append((stride, factor, lower_block, upper_block))
        diagonal, lower_block, upper_block, source = (
            next_diagonal,
            next_lower,
            next_upper,
            next_source,
        )
        stride = stride * 2
    last_factor = jnp.linalg.cholesky(diagonal)
    return (chol_apply(last_factor, source), stored, last_factor)


def per_device(
    ham_noise,
    channel_levels,
    coupling_noise,
    corr_weight,
    corr_basis,
    projector,
    energy_shift,
    sources,
    target,
    open_channels,
):
    channels = ham_noise.shape[1]
    energies = energy_shift.shape[0]
    identity = jnp.eye(channels, dtype=jnp.float32)
    element = lax.axis_index("elem")
    potential = jnp.dot(
        corr_basis, corr_basis.T, precision=FULL_PRECISION, preferred_element_type=jnp.float32
    )
    common = (
        0.5 * (ham_noise[0] + ham_noise[0].T)
        + (2.0 + channel_levels[0])[:, None] * identity
        + corr_weight[0] * potential
    )
    diagonal = common[None] + energy_shift[:, None, None] * identity
    lower_own = -(identity + coupling_noise[0]) * (element > 0).astype(jnp.float32)
    upper_own = from_behind(lower_own, "elem", -1).T
    lower_block = jnp.broadcast_to(lower_own, (energies, channels, channels))
    upper_block = jnp.broadcast_to(upper_own, (energies, channels, channels))
    wave = sources[:, 0]
    wave, stored, last_factor = eliminate(diagonal, lower_block, upper_block, wave)
    projector_own = projector[0]
    total_rows = projector_own.shape[1]
    rhs_width = wave.shape[2]
    share_rows = total_rows // lax.axis_size("elem")
    column_index = lax.axis_index("rhs") * rhs_width + jnp.arange(rhs_width)
    column_open = column_index[None, :] < open_channels[:, None]
    partial_k = jnp.einsum(
        "br,ebs->ers",
        projector_own,
        wave,
        precision=FULL_PRECISION,
        preferred_element_type=jnp.float32,
    )
    k_total = lax.psum(partial_k, "elem")
    row_open = jnp.arange(total_rows)[None, :] < open_channels[:, None]
    open_mask = (row_open[:, :, None] & column_open[:, None, :]).astype(jnp.float32)
    residual = open_mask * (k_total - target)
    k_share = lax.dynamic_slice_in_dim(k_total, element * share_rows, share_rows, 1)
    drive = PENALTY * wave + jnp.einsum(
        "br,ers->ebs",
        projector_own,
        residual,
        precision=FULL_PRECISION,
        preferred_element_type=jnp.float32,
    )
    for stride, factor, lower_saved, upper_saved in stored:
        solved = chol_apply(factor, drive)
        from_below = from_behind(solved, "elem", stride)
        from_above = from_behind(solved, "elem", -stride)
        drive = drive - matmul(lower_saved, from_below) - matmul(upper_saved, from_above)
    adjoint = chol_apply(last_factor, drive)
    side_wave = jnp.einsum(
        "ebs,bm->esm",
        wave,
        corr_basis,
        precision=FULL_PRECISION,
        preferred_element_type=jnp.float32,
    )
    side_adjoint = jnp.einsum(
        "ebs,bm->esm",
        adjoint,
        corr_basis,
        precision=FULL_PRECISION,
        preferred_element_type=jnp.float32,
    )
    local_term = corr_weight[0] * (
        jnp.einsum(
            "ebs,esm->bm",
            adjoint,
            side_wave,
            precision=FULL_PRECISION,
            preferred_element_type=jnp.float32,
        )
        + jnp.einsum(
            "ebs,esm->bm",
            wave,
            side_adjoint,
            precision=FULL_PRECISION,
            preferred_element_type=jnp.float32,
        )
    )
    scale_total = energies * lax.axis_size("energy") * lax.axis_size("elem")
    basis_grad = -lax.psum(local_term, ("elem", "energy", "rhs")) / scale_total
    return (wave[:, None], adjoint[:, None], k_share, basis_grad)


def solution(mesh):
    return jax.shard_map(
        per_device,
        mesh=mesh,
        in_specs=(
            P(("groups", "elem"), None, None),
            P(("groups", "elem"), None),
            P(("groups", "elem"), None, None),
            P(("groups", "elem")),
            P("groups", None),
            P(("groups", "elem"), None, None),
            P(("groups", "energy")),
            P(("groups", "energy"), "elem", None, "rhs"),
            P(("groups", "energy"), None, "rhs"),
            P(("groups", "energy")),
        ),
        out_specs=(
            P(("groups", "energy"), "elem", None, "rhs"),
            P(("groups", "energy"), "elem", None, "rhs"),
            P(("groups", "energy"), "elem", "rhs"),
            P("groups", None),
        ),
        check_vma=False,
    )
```

profile of v0, /device:TPU:0, one launch (start us, length us, event | category | flops | bytes accessed | tf_op | source)
XLA Modules:
  0.0 444.3 jit_solution(15673696793555747466)
XLA Ops:
  12.0 11.7 %custom-call.36 = f32[1,128,128]{2,1,0:T(8,128)S(1)} custom-call(f32[1,128,128]{2,1,0:T(8,128)S(1)} %cholesky.265), custom_call_target="Cholesky" | custom-call | tf_op jit(solution)/shard_map/jit(cholesky)/cholesky | solution.py:39
  23.7 9.8 %custom-call.37 = f32[1,1,128,128]{2,3,1,0:T(8,128)S(1)} custom-call(f32[1,1,128,128]{3,2,1,0:T(8,128)S(1)} %get-tuple-element.146), custom_call_target="InvertDiagBlocksLowerTriangular" | custom-call | tf_op jit(solution)/shard_map/jit(cholesky)/cholesky | solution.py:39
  34.1 11.7 %custom-call.38 = f32[1,128,128]{2,1,0:T(8,128)S(1)} custom-call(f32[1,128,128]{2,1,0:T(8,128)S(1)} %fusion.19), custom_call_target="Cholesky" | custom-call | tf_op jit(solution)/shard_map/jit(cholesky)/cholesky | solution.py:39
  47.9 15.7 %while.24 = (s32[]{:T(128)}, f32[1,256,256]{2,1,0:T(8,128)S(1)}, s32[2,2]{1,0:T(2,128)S(1)}, f32[2,1,128,128]{3,2,1,0:T(8,128)S(1)}, s32[]{:T(128)}) while((s32[]{:T(128)}, f32[1,256,256]{2,1,0:T(8,128)S(1)}, s32[2,2]{1,0:T(2,128)S(1)}, f32[2,1,128,128]{3,2,1,0:T(8,128)S(1)}, s32[]{:T(128)}) %tuple.98), condition=%wide.while_cond.1, body=%wide.while_body.1.sunk | while | flops 2 | bytes 131189 | solution.py:18
  63.5 19.7 %custom-call.40 = f32[1,2,128,128]{2,3,1,0:T(8,128)S(1)} custom-call(f32[1,2,128,128]{3,2,1,0:T(8,128)S(1)} %bitcast.567), custom_call_target="InvertDiagBlocksLowerTriangular" | custom-call | tf_op jit(solution)/shard_map/triangular_solve/custom-call.4 | solution.py:18
  88.3 7.0 %collective-permute-start.1 = (f32[1,256,640]{2,1,0:T(8,128)S(1)}, f32[1,256,640]{2,1,0:T(8,128)}, u32[]{:S(2)}, u32[]{:S(2)}) collective-permute-start(f32[1,256,640]{2,1,0:T(8,128)S(1)} %pad_maximum_fusion.1), channel_id=1, source_target_pairs={{0,4},{4,8},{8,12},{1,5},{5,9},{9,13},{2,6},{6,10},{10,14},{3,7},{... | collective-permute-start | bytes 1966088 | tf_op jit(solution)/shard_map/ppermute | solution.py:13
  95.4 11.9 %collective-permute-done.2 = f32[1,256,640]{2,1,0:T(8,128)S(1)} collective-permute-done((f32[1,256,640]{2,1,0:T(8,128)S(1)}, f32[1,256,640]{2,1,0:T(8,128)S(1)}, u32[]{:S(2)}, u32[]{:S(2)}) %collective-permute-start.2) | collective-permute-done | bytes 655392 | tf_op jit(solution)/shard_map/ppermute | solution.py:13
  110.2 11.7 %custom-call.41 = f32[1,128,128]{2,1,0:T(8,128)S(1)} custom-call(f32[1,128,128]{2,1,0:T(8,128)S(1)} %cholesky.268), custom_call_target="Cholesky" | custom-call | tf_op jit(solution)/shard_map/jit(cholesky)/cholesky | solution.py:39
  122.6 9.8 %custom-call.42 = f32[1,1,128,128]{2,3,1,0:T(8,128)S(1)} custom-call(f32[1,1,128,128]{3,2,1,0:T(8,128)S(1)} %get-tuple-element.142), custom_call_target="InvertDiagBlocksLowerTriangular" | custom-call | tf_op jit(solution)/shard_map/jit(cholesky)/cholesky | solution.py:39
  132.9 11.7 %custom-call.43 = f32[1,128,128]{2,1,0:T(8,128)S(1)} custom-call(f32[1,128,128]{2,1,0:T(8,128)S(1)} %fusion.20), custom_call_target="Cholesky" | custom-call | tf_op jit(solution)/shard_map/jit(cholesky)/cholesky | solution.py:39
  146.6 4.2 while.25
  150.8 19.7 %custom-call.45 = f32[1,2,128,128]{2,3,1,0:T(8,128)S(1)} custom-call(f32[1,2,128,128]{3,2,1,0:T(8,128)S(1)} %bitcast.568), custom_call_target="InvertDiagBlocksLowerTriangular" | custom-call | tf_op jit(solution)/shard_map/triangular_solve/custom-call.4 | solution.py:18
  178.8 7.7 %collective-permute-start.3 = (f32[1,256,640]{2,1,0:T(8,128)S(1)}, f32[1,256,640]{2,1,0:T(8,128)}, u32[]{:S(2)}, u32[]{:S(2)}) collective-permute-start(f32[1,256,640]{2,1,0:T(8,128)S(1)} %pad_maximum_fusion.3), channel_id=1, source_target_pairs={{0,8},{4,12},{1,9},{5,13},{2,10},{6,14},{3,11},{7,15},{16,24},{20,... | collective-permute-start | bytes 1966088 | tf_op jit(solution)/shard_map/ppermute | solution.py:13
  187.2 23.0 %collective-permute-done.4 = f32[1,256,640]{2,1,0:T(8,128)} collective-permute-done((f32[1,256,640]{2,1,0:T(8,128)S(1)}, f32[1,256,640]{2,1,0:T(8,128)}, u32[]{:S(2)}, u32[]{:S(2)}) %collective-permute-start.4) | collective-permute-done | bytes 655392 | tf_op jit(solution)/shard_map/ppermute | solution.py:13
  211.8 1.6 fusion.7
  213.6 11.7 %custom-call.46 = f32[1,128,128]{2,1,0:T(8,128)S(1)} custom-call(f32[1,128,128]{2,1,0:T(8,128)S(1)} %cholesky.271), custom_call_target="Cholesky" | custom-call | tf_op jit(solution)/shard_map/jit(cholesky)/cholesky | solution.py:63
  226.0 9.8 %custom-call.47 = f32[1,1,128,128]{2,3,1,0:T(8,128)S(1)} custom-call(f32[1,1,128,128]{3,2,1,0:T(8,128)S(1)} %get-tuple-element.138), custom_call_target="InvertDiagBlocksLowerTriangular" | custom-call | tf_op jit(solution)/shard_map/jit(cholesky)/cholesky | solution.py:63
  236.3 11.7 %custom-call.48 = f32[1,128,128]{2,1,0:T(8,128)S(1)} custom-call(f32[1,128,128]{2,1,0:T(8,128)S(1)} %fusion.21), custom_call_target="Cholesky" | custom-call | tf_op jit(solution)/shard_map/jit(cholesky)/cholesky | solution.py:63
  250.0 4.2 while.26
  254.2 19.7 %custom-call.50 = f32[1,2,128,128]{2,3,1,0:T(8,128)S(1)} custom-call(f32[1,2,128,128]{3,2,1,0:T(8,128)S(1)} %bitcast.566), custom_call_target="InvertDiagBlocksLowerTriangular" | custom-call | tf_op jit(solution)/shard_map/triangular_solve/custom-call.6 | solution.py:18
  280.6 35.8 %all-reduce.4.cloned.1.call-done = f32[1,256,128]{1,2,0:T(8,128)} async-done(((f32[1,256,128]{1,2,0:T(8,128)}), f32[1,256,128]{1,2,0:T(8,128)}) %all-reduce.4.cloned.1.call-update) | async-done | bytes 131088 | tf_op jit(solution)/shard_map/psum | solution.py:111
  320.7 4.6 %collective-permute-start.5 = (f32[1,256,128]{2,1,0:T(8,128)S(1)}, f32[1,256,128]{2,1,0:T(8,128)S(1)}, u32[]{:S(2)}, u32[]{:S(2)}) collective-permute-start(f32[1,256,128]{2,1,0:T(8,128)S(1)} %pad_maximum_fusion.5), channel_id=1, source_target_pairs={{0,4},{4,8},{8,12},{1,5},{5,9},{9,13},{2,6},{6,10},{10,14},{3,7},{... | collective-permute-start | bytes 393224 | tf_op jit(solution)/shard_map/ppermute | solution.py:13
  331.3 5.5 %collective-permute-start.7 = (f32[1,256,128]{2,1,0:T(8,128)S(1)}, f32[1,256,128]{2,1,0:T(8,128)S(1)}, u32[]{:S(2)}, u32[]{:S(2)}) collective-permute-start(f32[1,256,128]{2,1,0:T(8,128)S(1)} %pad_maximum_fusion.6), channel_id=1, source_target_pairs={{0,8},{4,12},{1,9},{5,13},{2,10},{6,14},{3,11},{7,15},{16,24},{20,... | collective-permute-start | bytes 393224 | tf_op jit(solution)/shard_map/ppermute | solution.py:13
  345.7 89.8 %all-reduce.6.cloned.1.call-done = f32[256,256]{0,1:T(8,128)} async-done(((f32[256,256]{0,1:T(8,128)}), f32[256,256]{0,1:T(8,128)}) %all-reduce.6.cloned.1.call-update) | async-done | bytes 262160 | tf_op jit(solution)/shard_map/psum | solution.py:160
  (164 shorter events, 65.6 us)
Async XLA Ops:
  7.2 4.2 copy-start
  7.2 309.3 %all-reduce.4.cloned.1.call-start = ((), (), s32[]{:S(2)}) async-start(), calls=%async_computation | async-start | bytes 262144 | tf_op jit(solution)/shard_map/psum | solution.py:111
  8.4 2.8 copy-start.1
  8.4 74.9 %collective-permute-start = (f32[256,256]{0,1:T(8,128)S(1)}, f32[256,256]{0,1:T(8,128)S(1)}, u32[]{:S(2)}, u32[]{:S(2)}) collective-permute-start(f32[256,256]{0,1:T(8,128)S(1)} %fusion.47), channel_id=1, source_target_pairs={{4,0},{8,4},{12,8},{5,1},{9,5},{13,9},{6,2},{10,6},{14,10},{7,3},{... | collective-permute-start | bytes 786440 | tf_op jit(solution)/shard_map/ppermute | solution.py:13
  10.5 0.7 copy-start.7
  47.9 35.4 %copy-start.2 = (f32[1,256,256]{2,1,0:T(8,128)S(1)}, f32[1,256,256]{2,1,0:T(8,128)}, u32[]{:S(2)}) copy-start(f32[1,256,256]{2,1,0:T(8,128)} %param.21) | copy-start | bytes 786436
  83.2 0.9 copy-start.4
  87.0 20.3 %collective-permute-start.2 = (f32[1,256,640]{2,1,0:T(8,128)S(1)}, f32[1,256,640]{2,1,0:T(8,128)S(1)}, u32[]{:S(2)}, u32[]{:S(2)}) collective-permute-start(f32[1,256,640]{2,1,0:T(8,128)S(1)} %pad_maximum_fusion.1), channel_id=1, source_target_pairs={{4,0},{8,4},{12,8},{5,1},{9,5},{13,9},{6,2},{10,6},{14,10},{7,3},{... | collective-permute-start | bytes 1966088 | tf_op jit(solution)/shard_map/ppermute | solution.py:13
  88.3 20.2 %collective-permute-start.1 = (f32[1,256,640]{2,1,0:T(8,128)S(1)}, f32[1,256,640]{2,1,0:T(8,128)}, u32[]{:S(2)}, u32[]{:S(2)}) collective-permute-start(f32[1,256,640]{2,1,0:T(8,128)S(1)} %pad_maximum_fusion.1), channel_id=1, source_target_pairs={{0,4},{4,8},{8,12},{1,5},{5,9},{9,13},{2,6},{6,10},{10,14},{3,7},{... | collective-permute-start | bytes 1966088 | tf_op jit(solution)/shard_map/ppermute | solution.py:13
  177.5 32.7 %collective-permute-start.4 = (f32[1,256,640]{2,1,0:T(8,128)S(1)}, f32[1,256,640]{2,1,0:T(8,128)}, u32[]{:S(2)}, u32[]{:S(2)}) collective-permute-start(f32[1,256,640]{2,1,0:T(8,128)S(1)} %pad_maximum_fusion.3), channel_id=1, source_target_pairs={{8,0},{12,4},{9,1},{13,5},{10,2},{14,6},{11,3},{15,7},{24,16},{28,... | collective-permute-start | bytes 1966088 | tf_op jit(solution)/shard_map/ppermute | solution.py:13
  178.8 33.0 %collective-permute-start.3 = (f32[1,256,640]{2,1,0:T(8,128)S(1)}, f32[1,256,640]{2,1,0:T(8,128)}, u32[]{:S(2)}, u32[]{:S(2)}) collective-permute-start(f32[1,256,640]{2,1,0:T(8,128)S(1)} %pad_maximum_fusion.3), channel_id=1, source_target_pairs={{0,8},{4,12},{1,9},{5,13},{2,10},{6,14},{3,11},{7,15},{16,24},{20,... | collective-permute-start | bytes 1966088 | tf_op jit(solution)/shard_map/ppermute | solution.py:13
  277.6 1.0 copy-start.3
  279.6 0.9 copy-start.6
  279.6 155.8 %all-reduce.6.cloned.1.call-start = ((), (), s32[]{:S(2)}) async-start(), calls=%async_computation.1 | async-start | bytes 524288 | tf_op jit(solution)/shard_map/psum | solution.py:160
  319.4 6.9 %collective-permute-start.6 = (f32[1,256,128]{2,1,0:T(8,128)S(1)}, f32[1,256,128]{2,1,0:T(8,128)S(1)}, u32[]{:S(2)}, u32[]{:S(2)}) collective-permute-start(f32[1,256,128]{2,1,0:T(8,128)S(1)} %pad_maximum_fusion.5), channel_id=1, source_target_pairs={{4,0},{8,4},{12,8},{5,1},{9,5},{13,9},{6,2},{10,6},{14,10},{7,3},{... | collective-permute-start | bytes 393224 | tf_op jit(solution)/shard_map/ppermute | solution.py:13
  320.7 7.1 %collective-permute-start.5 = (f32[1,256,128]{2,1,0:T(8,128)S(1)}, f32[1,256,128]{2,1,0:T(8,128)S(1)}, u32[]{:S(2)}, u32[]{:S(2)}) collective-permute-start(f32[1,256,128]{2,1,0:T(8,128)S(1)} %pad_maximum_fusion.5), channel_id=1, source_target_pairs={{0,4},{4,8},{8,12},{1,5},{5,9},{9,13},{2,6},{6,10},{10,14},{3,7},{... | collective-permute-start | bytes 393224 | tf_op jit(solution)/shard_map/ppermute | solution.py:13
  329.6 7.8 %collective-permute-start.8 = (f32[1,256,128]{2,1,0:T(8,128)S(1)}, f32[1,256,128]{2,1,0:T(8,128)S(1)}, u32[]{:S(2)}, u32[]{:S(2)}) collective-permute-start(f32[1,256,128]{2,1,0:T(8,128)S(1)} %pad_maximum_fusion.6), channel_id=1, source_target_pairs={{8,0},{12,4},{9,1},{13,5},{10,2},{14,6},{11,3},{15,7},{24,16},{28,... | collective-permute-start | bytes 393224 | tf_op jit(solution)/shard_map/ppermute | solution.py:13
  331.3 8.0 %collective-permute-start.7 = (f32[1,256,128]{2,1,0:T(8,128)S(1)}, f32[1,256,128]{2,1,0:T(8,128)S(1)}, u32[]{:S(2)}, u32[]{:S(2)}) collective-permute-start(f32[1,256,128]{2,1,0:T(8,128)S(1)} %pad_maximum_fusion.6), channel_id=1, source_target_pairs={{0,8},{4,12},{1,9},{5,13},{2,10},{6,14},{3,11},{7,15},{16,24},{20,... | collective-permute-start | bytes 393224 | tf_op jit(solution)/shard_map/ppermute | solution.py:13
  343.3 0.9 copy-start.5
Sparse Core Ops, SparseCore 0:
  279.7 36.6 all-reduce.3
  343.5 91.9 all-reduce.5
where the time goes:
time: 447 us; the launch traced here: 444 us
  other arithmetic  165 us (37%)
  waiting for transfers between devices  164 us (37%)
  matrix products  31.8 us (7%)
  starting transfers between devices  31.4 us (7%)
  between operations  21 us (5%)
  local copies, waits for them, and re-layouts  18.5 us (4%)
  loops' own time  12.2 us (3%)
    psum x1, waiting for transfers between devices, per_device(): basis_grad = -lax.psum(local_term, ('elem', 'energy', 'rhs')) / scale_total  89.8 us
    another operation x13, other arithmetic, eliminate(): factor = jnp.linalg.cholesky(diagonal)  68.5 us
    another operation x11, other arithmetic, chol_apply(): lax.linalg.triangular_solve(factor, halfway, left_side=True, lower=True,...  59.2 us
    ppermute x9, waiting for transfers between devices, from_behind(): lax.ppermute(value, axis, [(source, source + steps) for source in range(f...  38.8 us
    psum x1, waiting for transfers between devices, per_device(): k_total = lax.psum(partial_k, 'elem')  35.8 us
    another operation x7, other arithmetic, eliminate(): last_factor = jnp.linalg.cholesky(diagonal)  34.6 us
    ppermute x9, starting transfers between devices, from_behind(): lax.ppermute(value, axis, [(source, source + steps) for source in range(f...  31.4 us
    dot_general x14, matrix products, matmul(): jnp.einsum('eij,ejk->eik', lhs_block, rhs_block, precision=FULL_PRECISION...  13.6 us
  transfers between devices with their start and end apart: 11, of which 8 were waited for; matrix products, arithmetic and copies ran while one was open for 15% of the time, Pallas kernels for 0%

commit v1 on v0

v1 whole, which is shorter than its diff:
```python
import functools

import jax
import jax.numpy as jnp
from jax import lax
from jax.experimental import pallas as pl
from jax.experimental.pallas import tpu as pltpu
from jax.sharding import PartitionSpec as P

PENALTY = 0.5
STEPS = 3
START_SCALE = 1.75
RESIDUAL_BOUND = 0.01
F32 = jnp.float32
BF16 = jnp.bfloat16
NN = (((1,), (0,)), ((), ()))
NT = (((1,), (1,)), ((), ()))
VMEM_BYTES = 48 * 1024 * 1024


def split(value):
    high = value.astype(BF16)
    return high, (value - high.astype(F32)).astype(BF16)


def dot1(lhs, rhs, dims=NN):
    return lax.dot_general(lhs, rhs, dims, preferred_element_type=F32)


def dot3(lhs, rhs, dims=NN):
    return (
        dot1(lhs[0], rhs[0], dims) + dot1(lhs[0], rhs[1], dims) + dot1(lhs[1], rhs[0], dims)
    )


def eye_of(size):
    rows = lax.broadcasted_iota(jnp.int32, (size, size), 0)
    columns = lax.broadcasted_iota(jnp.int32, (size, size), 1)
    return (rows == columns).astype(F32)


def row_norm(matrix):
    return jnp.max(jnp.sum(jnp.abs(matrix), axis=1, keepdims=True), axis=0, keepdims=True)


def fast_inverse(matrix, identity):
    scale = START_SCALE / row_norm(matrix)
    error = identity - scale * matrix
    inverse = scale * (identity + error)
    error16 = error.astype(BF16)
    for _ in range(STEPS):
        error16 = dot1(error16, error16).astype(BF16)
        inverse = inverse + dot1(inverse.astype(BF16), error16)
    parts = split(inverse)
    residual = identity - dot3(split(matrix), parts)
    inverse = inverse + dot1(parts[0], residual.astype(BF16))
    return inverse, row_norm(residual)


def exact_dot(lhs, rhs):
    return lax.dot_general(
        lhs, rhs, NN, precision=lax.Precision.HIGHEST, preferred_element_type=F32
    )


def slow_inverse(matrix, identity, matrix_scr, inverse_scr):
    matrix_scr[...] = matrix
    inverse_scr[...] = identity * (START_SCALE / row_norm(matrix))

    def going(state):
        count, size = state
        return (size > 1e-3) & (count < 100)

    def step(state):
        count, _ = state
        inverse = inverse_scr[...]
        residual = identity - exact_dot(matrix_scr[...], inverse)
        inverse_scr[...] = inverse + exact_dot(inverse, residual)
        return count + 1, jnp.max(row_norm(residual))

    lax.while_loop(going, step, (jnp.int32(0), jnp.float32(1e9)))
    return inverse_scr[...], jnp.zeros((1, 1), F32)


def factor_kernel(
    shift_ref, weight_ref, level_ref, ham_ref, coupling_ref, basis_ref, inverse_ref, link_ref,
    diag_scr, matrix_scr, inverse_scr,
):
    count = ham_ref.shape[0]
    size = ham_ref.shape[1]
    middle = count // 2
    identity = eye_of(size)
    basis = split(basis_ref[...])
    potential = dot3(basis, basis, NT)
    for n in range(count):
        ham = ham_ref[n]
        diag_scr[n] = (
            0.5 * (ham + ham.T)
            + (2.0 + level_ref[n : n + 1, :] + shift_ref[0]) * identity
            + weight_ref[n] * potential
        )

    def eliminate(invert):
        worst = jnp.zeros((1, 1), F32)
        forward = diag_scr[0]
        backward = diag_scr[count - 1]

        def finish(n, matrix, worst):
            inverse, size_left = invert(matrix, identity)
            parts = split(inverse)
            inverse_ref[0, n] = parts[0]
            inverse_ref[1, n] = parts[1]
            return parts, jnp.maximum(worst, size_left)

        def keep(n, link):
            parts = split(link)
            link_ref[0, n] = parts[0]
            link_ref[1, n] = parts[1]
            return parts

        meeting = diag_scr[middle]
        for step in range(max(middle, count - 1 - middle)):
            ahead, behind = step, count - 1 - step
            if ahead < middle:
                parts, worst = finish(ahead, forward, worst)
                coupling = split(-(identity + coupling_ref[ahead + 1]))
                link = keep(ahead + 1, dot3(coupling, parts))
                update = dot3(link, coupling, NT)
                if ahead + 1 < middle:
                    forward = diag_scr[ahead + 1] - update
                else:
                    meeting = meeting - update
            if behind > middle:
                parts, worst = finish(behind, backward, worst)
                raw = -(identity + coupling_ref[behind])
                link = keep(behind, dot3(split(raw.T), parts))
                update = dot3(link, split(raw))
                if behind - 1 > middle:
                    backward = diag_scr[behind - 1] - update
                else:
                    meeting = meeting - update
        _, worst = finish(middle, meeting, worst)
        return worst

    worst = jnp.max(eliminate(fast_inverse))

    @pl.when(jnp.logical_not(worst <= RESIDUAL_BOUND))
    def _():
        eliminate(
            functools.partial(slow_inverse, matrix_scr=matrix_scr, inverse_scr=inverse_scr)
        )


def factorize(shift, weights, levels, ham, coupling, basis):
    count, size = ham.shape[0], ham.shape[1]
    smem = pl.BlockSpec(memory_space=pltpu.SMEM)
    vmem = pl.BlockSpec(memory_space=pltpu.VMEM)
    half = jax.ShapeDtypeStruct((2, count, size, size), BF16)
    return pl.pallas_call(
        factor_kernel,
        out_shape=(half, half),
        in_specs=[smem, smem, vmem, vmem, vmem, vmem],
        out_specs=(vmem, vmem),
        scratch_shapes=[
            pltpu.VMEM((count, size, size), F32),
            pltpu.VMEM((size, size), F32),
            pltpu.VMEM((size, size), F32),
        ],
        compiler_params=pltpu.CompilerParams(vmem_limit_bytes=VMEM_BYTES),
        name="factorize",
    )(shift, weights, levels, ham, coupling, basis)


def solve_kernel(
    place_ref, open_ref, weight_ref, inverse_ref, link_ref, source_ref, projector_ref,
    target_ref, wave_ref, adjoint_ref, share_ref, gram_ref, own_scr, k_scr,
):
    count = source_ref.shape[0]
    channels, width = source_ref.shape[1:]
    middle = count // 2
    me, column = place_ref[0], place_ref[1]
    inverses = [(inverse_ref[0, n], inverse_ref[1, n]) for n in range(count)]
    links = [(link_ref[0, n], link_ref[1, n]) if n != 0 else None for n in range(count)]
    projectors = [split(projector_ref[n]) for n in range(count)]

    def solve(blocks):
        reduced = list(blocks)
        for n in range(1, middle + 1):
            reduced[n] = reduced[n] - dot3(split(reduced[n - 1]), links[n], NT)
        for n in range(count - 1, middle, -1):
            reduced[n - 1] = reduced[n - 1] - dot3(split(reduced[n]), links[n], NT)
        solved = [dot3(split(reduced[n]), inverses[n]) for n in range(count)]
        halves = [None] * count
        halves[middle] = split(solved[middle])
        for n in range(middle, 0, -1):
            solved[n - 1] = solved[n - 1] - dot3(halves[n], links[n])
            halves[n - 1] = split(solved[n - 1])
        for n in range(middle + 1, count):
            solved[n] = solved[n] - dot3(halves[n - 1], links[n])
            halves[n] = split(solved[n])
        return solved, halves

    wave, wave_halves = solve([source_ref[n].T for n in range(count)])
    k_total = dot3(wave_halves[0], projectors[0])
    for n in range(1, count):
        k_total = k_total + dot3(wave_halves[n], projectors[n])
    k_rows = lax.broadcasted_iota(jnp.int32, k_total.shape, 1)
    k_columns = lax.broadcasted_iota(jnp.int32, k_total.shape, 0) + column * width
    opened = (k_rows < open_ref[0]) & (k_columns < open_ref[0])
    residual = split(jnp.where(opened, k_total - target_ref[...].T, 0.0))
    drive = [PENALTY * wave[n] + dot3(residual, projectors[n], NT) for n in range(count)]
    adjoint, _ = solve(drive)

    share = share_ref.shape[0]
    k_scr[...] = k_total.T
    share_ref[...] = k_scr[pl.ds(pl.multiple_of(me * share, share), share), :]
    wave = [value.T for value in wave]
    adjoint = [value.T for value in adjoint]
    for n in range(count):
        own_scr[n] = wave[n]
    wave_ref[...] = own_scr[me]
    for n in range(count):
        own_scr[n] = adjoint[n]
    adjoint_ref[...] = own_scr[me]
    weighted = jnp.concatenate([weight_ref[n] * wave[n] for n in range(count)], axis=1)
    gram = dot3(split(jnp.concatenate(adjoint, axis=1)), split(weighted), NT)
    gram_ref[...] = gram + gram.T


def solve_all(place, opened, weights, inverses, links, sources, projectors, target):
    count, channels, width = sources.shape
    rows = target.shape[0]
    smem = pl.BlockSpec(memory_space=pltpu.SMEM)
    vmem = pl.BlockSpec(memory_space=pltpu.VMEM)
    return pl.pallas_call(
        solve_kernel,
        out_shape=(
            jax.ShapeDtypeStruct((channels, width), F32),
            jax.ShapeDtypeStruct((channels, width), F32),
            jax.ShapeDtypeStruct((rows // count, width), F32),
            jax.ShapeDtypeStruct((channels, channels), F32),
        ),
        in_specs=[smem, smem, smem, vmem, vmem, vmem, vmem, vmem],
        out_specs=(vmem,) * 4,
        scratch_shapes=[
            pltpu.VMEM((count, channels, width), F32),
            pltpu.VMEM((rows, width), F32),
        ],
        compiler_params=pltpu.CompilerParams(vmem_limit_bytes=VMEM_BYTES),
        name="solve",
    )(place, opened, weights, inverses, links, sources, projectors, target)


def total_over(value, axis):
    count = lax.axis_size(axis)
    if count & (count - 1):
        return lax.psum(value, axis)
    step = 1
    while step < count:
        value = value + lax.ppermute(value, axis, [(i, i ^ step) for i in range(count)])
        step = step * 2
    return value


def per_device(
    ham_noise,
    channel_levels,
    coupling_noise,
    corr_weight,
    corr_basis,
    projector,
    energy_shift,
    sources,
    target,
    open_channels,
):
    elements = lax.axis_size("elem")
    size = ham_noise.shape[1]
    extra = jnp.concatenate(
        [channel_levels, jnp.broadcast_to(corr_weight[:, None], (7, size))], axis=0
    )
    matrices = jnp.concatenate([ham_noise[0], coupling_noise[0], extra], axis=0)
    matrices = lax.all_gather(matrices, "elem")
    source_all = lax.all_gather(sources[0, 0], "elem")
    projector_all = lax.all_gather(projector[0], "elem")
    ham = matrices[:, :size]
    coupling = matrices[:, size : 2 * size]
    levels = matrices[:, 2 * size]
    weights = matrices[:, 2 * size + 1, 0]
    inverses, links = factorize(energy_shift, weights, levels, ham, coupling, corr_basis)
    place = jnp.stack([lax.axis_index("elem"), lax.axis_index("rhs")]).astype(jnp.int32)
    wave, adjoint, share, gram = solve_all(
        place, open_channels, weights, inverses, links, source_all, projector_all, target[0]
    )
    gram = total_over(total_over(gram, "rhs"), "energy")
    grad = jnp.dot(gram, corr_basis, precision=lax.Precision.HIGHEST)
    basis_grad = grad * (-1.0 / (lax.axis_size("energy") * elements))
    return wave[None, None], adjoint[None, None], share[None], basis_grad


def solution(mesh):
    return jax.shard_map(
        per_device,
        mesh=mesh,
        in_specs=(
            P(("groups", "elem"), None, None),
            P(("groups", "elem"), None),
            P(("groups", "elem"), None, None),
            P(("groups", "elem")),
            P("groups", None),
            P(("groups", "elem"), None, None),
            P(("groups", "energy")),
            P(("groups", "energy"), "elem", None, "rhs"),
            P(("groups", "energy"), None, "rhs"),
            P(("groups", "energy")),
        ),
        out_specs=(
            P(("groups", "energy"), "elem", None, "rhs"),
            P(("groups", "energy"), "elem", None, "rhs"),
            P(("groups", "energy"), "elem", "rhs"),
            P("groups", None),
        ),
        check_vma=False,
    )
```

time: 447 us -> 117 us (0.26)
  other arithmetic: 165 us -> 2.11 us
  waiting for transfers between devices: 164 us -> 56 us
  matrix products: 31.8 us -> 1.09 us
  starting transfers between devices: 31.4 us -> 1.62 us
  blocking collectives: 0 us -> 22.6 us
  local copies, waits for them, and re-layouts: 18.5 us -> 4.59 us
  Pallas kernels: 0 us -> 12.6 us
  loops' own time: 12.2 us -> 0 us
  between operations: 21 us -> 16 us
    another operation x31 -> x1, other arithmetic: 162 us -> 0.08 us  [per_device(): jnp.stack([lax.axis_index('elem'), lax.axis_index('rhs')]).astype(jnp.int32)]
    psum x2 -> x0, waiting for transfers between devices: 126 us -> none  [the longest x1 89.8 us: per_device(): basis_grad = -lax.psum(local_term, ('elem', 'energy', 'rhs')) / scale_total]
    all_gather x0 -> x2, waiting for transfers between devices: none -> 46.9 us  [the longest x1 28.5 us: per_device(): matrices = lax.all_gather(matrices, 'elem')]
    ppermute x9 -> x2, waiting for transfers between devices: 38.8 us -> 8.41 us  [total_over(): lax.ppermute(value, axis, [(i, i ^ step) for i in range(count)])]
    ppermute x9 -> x2, starting transfers between devices: 31.4 us -> 1.54 us  [total_over(): lax.ppermute(value, axis, [(i, i ^ step) for i in range(count)])]
    all_gather x0 -> x1, blocking collectives: none -> 22.6 us  [per_device(): source_all = lax.all_gather(sources[0, 0], 'elem')]
    dot_general x21 -> x1, matrix products: 18.7 us -> 1.09 us  [per_device(): grad = jnp.dot(gram, corr_basis, precision=lax.Precision.HIGHEST)]
    another operation x42 -> x0, matrix products: 13 us -> none  [the longest x18 6.23 us: chol_apply(): lax.linalg.triangular_solve(factor, values, left_side=True, lower=True)]
  transfers between devices with their start and end apart: 11 -> 4, of which waited for: 8 -> 4; matrix products, arithmetic and copies ran while one was open for 15% -> 3% of each run, Pallas kernels for 0% -> 7%
where the time goes in v1:
time: 117 us
  waiting for transfers between devices  56 us (48%)
  blocking collectives  22.6 us (19%)
  between operations  16 us (14%)
  Pallas kernels  12.6 us (11%)
  local copies, waits for them, and re-layouts  4.59 us (4%)
  other arithmetic  2.11 us (2%)
  starting transfers between devices  1.62 us (1%)
    all_gather x1, waiting for transfers between devices, per_device(): matrices = lax.all_gather(matrices, 'elem')  28.5 us
    all_gather x1, blocking collectives, per_device(): source_all = lax.all_gather(sources[0, 0], 'elem')  22.6 us
    all_gather x1, waiting for transfers between devices, per_device(): projector_all = lax.all_gather(projector[0], 'elem')  18.4 us
    ppermute x2, waiting for transfers between devices, total_over(): lax.ppermute(value, axis, [(i, i ^ step) for i in range(count)])  8.41 us
    pallas_call x1, Pallas kernels, factorize(): pl.pallas_call(factor_kernel, out_shape=(half, half), in_specs=[smem, sme...  7.73 us
    pallas_call x1, Pallas kernels, solve_all(): pl.pallas_call(solve_kernel, out_shape=(jax.ShapeDtypeStruct((channels, w...  4.9 us
  transfers between devices with their start and end apart: 4, of which 4 were waited for; matrix products, arithmetic and copies ran while one was open for 3% of the time, Pallas kernels for 7%

profile of v1, /device:TPU:0, one launch (start us, length us, event | category | flops | bytes accessed | tf_op | source)
XLA Modules:
  0.0 116.6 jit_solution(18315957139374699020)
XLA Ops:
  7.2 0.0 all-gather.7.cloned.1.call-start
  7.9 0.1 pad.3.clone
  7.9 2.0 %maximum_maximum_fusion = f32[520,256]{1,0:T(8,128)} fusion(f32[1,256]{1,0:T(1,128)} %param.11, f32[256,256]{1,0:T(8,128)} %bitcast.22, f32[256,256]{1,0:T(8,128)} %bitcast.23, f32[520]{0:T(1024)S(1)} %pad.3.clone), kind=kLoop, calls=%fused_computation.1 | loop fusion | flops 399360 | bytes 1059872 | tf_op jit(solution)/shard_map/concatenate | solution.py:282
  9.9 0.0 all-gather.7.cloned.1.call-update
  10.0 0.0 all-gather.5.cloned.1.call-start
  10.0 0.7 all-gather.5.cloned.1.call-update
  12.0 0.1 pad_add_fusion.place_ref
  12.1 22.6 %all-gather.1 = f32[4,1,256,128]{3,2,1,0:T(8,128)S(1)} all-gather(f32[1,1,256,128]{3,2,1,0:T(8,128)} %param.17), channel_id=3, replica_groups=mesh['groups'=2,'elem'=4,'energy'=2,'rhs'=2] {'elem'}, dimensions={0}, use_global_device_ids=true | all-gather | bytes 655360 | tf_op jit(solution)/shard_map/all_gather | solution.py:284
  34.7 28.5 %all-gather.7.cloned.1.call-done = f32[2080,256]{1,0:T(8,128)} async-done(((f32[520,256]{1,0:T(8,128)}), f32[2080,256]{1,0:T(8,128)}) %all-gather.7.cloned.1.call-update) | async-done | bytes 2129936 | tf_op jit(solution)/shard_map/all_gather | solution.py:283
  63.2 0.8 slice.17
  63.9 0.8 slice_reduce_fusion.weight_ref
  64.8 1.7 %fusion.1 = (f32[4,256,256]{2,1,0:T(8,128)S(1)}, f32[4,256,256]{2,1,0:T(8,128)S(1)}) fusion(f32[4,520,256]{2,1,0:T(8,128)} %bitcast.21), kind=kLoop, calls=%fused_computation.6 | loop fusion | bytes 4194304 | tf_op jit(solution)/shard_map/slice | solution.py:287
  66.4 0.0 copy-start.2
  66.5 0.0 copy-done.1
  66.5 7.7 %factorize.1 = (bf16[2,4,256,256]{3,2,1,0:T(8,128)(2,1)S(1)}, bf16[2,4,256,256]{3,2,1,0:T(8,128)(2,1)S(1)}) custom-call(f32[1]{0:T(128)S(6)} %copy.20.shift_ref, f32[4]{0:T(128)S(1)} %slice_reduce_fusion.weight_ref, f32[4,256]{1,0:T(4,128)S(1)} %bitcast.18, f32[4,256,256]{2,1,0:T(8,128)S(1)} %get-tuple-element.17.ham_ref, ...), custom_call_target="tpu_custom_call" | custom-call | tf_op jit(solution)/shard_map/factorize/pallas_call | solution.py:159
  74.2 18.4 %all-gather.5.cloned.1.call-done.projector_ref = f32[4,256,256]{2,1,0:T(8,128)} async-done(((f32[1,256,256]{2,1,0:T(8,128)}), f32[4,256,256]{2,1,0:T(8,128)}) %all-gather.5.cloned.1.call-update) | async-done | bytes 1048592 | tf_op jit(solution)/shard_map/all_gather | solution.py:285
  92.6 0.0 copy-done.2
  92.6 1.2 %copy-done = f32[4,256,256]{2,1,0:T(8,128)S(1)} copy-done((f32[4,256,256]{2,1,0:T(8,128)S(1)}, f32[4,256,256]{2,1,0:T(8,128)}, u32[]{:S(2)}) %copy-start) | copy-done | bytes 1048600
  93.8 4.9 %solve.1 = (f32[256,128]{1,0:T(8,128)}, f32[256,128]{1,0:T(8,128)}, f32[64,128]{1,0:T(8,128)}, f32[256,256]{1,0:T(8,128)S(1)}) custom-call(s32[2]{0:T(128)S(1)} %pad_add_fusion.place_ref, s32[1]{0:T(128)S(6)} %copy.21.open_ref, f32[4]{0:T(128)S(1)} %slice_reduce_fusion.weight_ref, bf16[2,4,256,256]{3,2,1,0:T(8,128)(2,1)S(1)} %get-tuple-element.10.inverse_ref, ...), custom_call_target="tpu_custom_call" | custom-call | tf_op jit(solution)/shard_map/solve/pallas_call | solution.py:235
  98.7 0.0 collective-permute-start
  98.7 1.5 %collective-permute-done = f32[256,256]{1,0:T(8,128)S(1)} collective-permute-done((f32[256,256]{1,0:T(8,128)S(1)}, f32[256,256]{1,0:T(8,128)S(1)}, u32[]{:S(2)}, u32[]{:S(2)}) %collective-permute-start) | collective-permute-done | bytes 262176 | tf_op jit(solution)/shard_map/ppermute | solution.py:260
  100.3 1.5 %collective-permute-start.1 = (f32[256,256]{1,0:T(8,128)S(1)}, f32[256,256]{1,0:T(8,128)S(1)}, u32[]{:S(2)}, u32[]{:S(2)}) collective-permute-start(f32[256,256]{1,0:T(8,128)S(1)} %add.6), channel_id=1, source_target_pairs={{0,2},{2,0},{1,3},{3,1},{4,6},{6,4},{5,7},{7,5},{8,10},{10,8},{9,1... | collective-permute-start | bytes 786440 | tf_op jit(solution)/shard_map/ppermute | solution.py:260
  101.8 6.9 %collective-permute-done.1 = f32[256,256]{1,0:T(8,128)S(1)} collective-permute-done((f32[256,256]{1,0:T(8,128)S(1)}, f32[256,256]{1,0:T(8,128)S(1)}, u32[]{:S(2)}, u32[]{:S(2)}) %collective-permute-start.1) | collective-permute-done | bytes 262176 | tf_op jit(solution)/shard_map/ppermute | solution.py:260
  108.7 1.1 convolution_multiply_fusion
  (5 shorter events, 0.0 us)
Async XLA Ops:
  7.2 56.0 %all-gather.7.cloned.1.call-start = ((), (), s32[]{:S(2)}) async-start(), calls=%async_computation.1 | async-start | bytes 2662400 | tf_op jit(solution)/shard_map/all_gather | solution.py:283
  10.0 82.6 %all-gather.5.cloned.1.call-start = ((), (), s32[]{:S(2)}) async-start(), calls=%async_computation | async-start | bytes 1310720 | tf_op jit(solution)/shard_map/all_gather | solution.py:285
  34.7 31.8 %copy-start.1 = (f32[256,256]{1,0:T(8,128)S(1)}, f32[256,256]{1,0:T(8,128)}, u32[]{:S(2)}) copy-start(f32[256,256]{1,0:T(8,128)} %basis_ref.1) | copy-start | bytes 786436
  66.4 26.2 %copy-start.2 = (f32[1,256,128]{2,1,0:T(8,128)S(1)}, f32[1,256,128]{2,1,0:T(8,128)}, u32[]{:S(2)}) copy-start(f32[1,256,128]{2,1,0:T(8,128)} %param.18) | copy-start | bytes 393220
  92.6 1.2 %copy-start = (f32[4,256,256]{2,1,0:T(8,128)S(1)}, f32[4,256,256]{2,1,0:T(8,128)}, u32[]{:S(2)}) copy-start(f32[4,256,256]{2,1,0:T(8,128)} %all-gather.5.cloned.1.call-done.projector_ref) | copy-start | bytes 3145732
  98.7 1.5 %collective-permute-start = (f32[256,256]{1,0:T(8,128)S(1)}, f32[256,256]{1,0:T(8,128)S(1)}, u32[]{:S(2)}, u32[]{:S(2)}) collective-permute-start(f32[256,256]{1,0:T(8,128)S(1)} %get-tuple-element.15), channel_id=1, source_target_pairs={{0,1},{1,0},{2,3},{3,2},{4,5},{5,4},{6,7},{7,6},{8,9},{9,8},{10,11... | collective-permute-start | bytes 786440 | tf_op jit(solution)/shard_map/ppermute | solution.py:260
  100.3 8.4 %collective-permute-start.1 = (f32[256,256]{1,0:T(8,128)S(1)}, f32[256,256]{1,0:T(8,128)S(1)}, u32[]{:S(2)}, u32[]{:S(2)}) collective-permute-start(f32[256,256]{1,0:T(8,128)S(1)} %add.6), channel_id=1, source_target_pairs={{0,2},{2,0},{1,3},{3,1},{4,6},{6,4},{5,7},{7,5},{8,10},{10,8},{9,1... | collective-permute-start | bytes 786440 | tf_op jit(solution)/shard_map/ppermute | solution.py:260
Sparse Core Ops, SparseCore 0:
  10.1 53.0 all-gather.6
  64.7 27.8 all-gather.4

commit v2 on v1

--- a/solution.py
+++ b/solution.py
@@ -82,22 +82,93 @@
     return inverse_scr[...], jnp.zeros((1, 1), F32)
 
 
+def pack_symmetric(matrix):
+    half = matrix.shape[0] // 2
+    rows = lax.broadcasted_iota(jnp.int32, (half, half), 0)
+    columns = lax.broadcasted_iota(jnp.int32, (half, half), 1)
+    first, second = matrix[:half, :half], matrix[half:, half:]
+    mixed = jnp.where(rows > columns, first, jnp.where(rows < columns, second, 0.0))
+    return jnp.concatenate([matrix[half:, :half], mixed], axis=1)
+
+
+def unpack_symmetric(packed):
+    half = packed.shape[0]
+    rows = lax.broadcasted_iota(jnp.int32, (half, half), 0)
+    columns = lax.broadcasted_iota(jnp.int32, (half, half), 1)
+    corner, mixed = packed[:, :half], packed[:, half:]
+    first = jnp.where(rows > columns, mixed, 0.0)
+    second = jnp.where(rows < columns, mixed, 0.0)
+    return jnp.concatenate(
+        [
+            jnp.concatenate([first + first.T, corner.T], axis=1),
+            jnp.concatenate([corner, second + second.T], axis=1),
+        ],
+        axis=0,
+    )
+
+
+def diagonal_of(matrix):
+    return jnp.sum(matrix * eye_of(matrix.shape[0]), axis=0, keepdims=True)
+
+
+def pack_kernel(
+    place_ref, weight_ref, level_ref, ham_ref, coupling_ref, projector_ref, matrix_ref,
+    part_ref, pack_scr,
+):
+    size = ham_ref.shape[0]
+    part = part_ref.shape[0]
+    ham_part = part // 2
+    ham = 0.5 * (ham_ref[...] + ham_ref[...].T)
+    pack_scr[...] = pack_symmetric(ham)
+    index = place_ref[0]
+    matrix_ref[:ham_part] = pack_scr[pl.ds(pl.multiple_of(index * ham_part, 8), ham_part), :]
+    rows = pl.ds(pl.multiple_of(index * part, 8), part)
+    matrix_ref[ham_part : ham_part + part] = coupling_ref[rows, :]
+    row = lax.broadcasted_iota(jnp.int32, (8, size), 0)
+    diagonal = diagonal_of(ham) + level_ref[...] + 2.0
+    matrix_ref[ham_part + part :] = jnp.where(row == 0, diagonal, weight_ref[0])
+    part_ref[...] = projector_ref[rows, :]
+
+
+def pack(place, weight, level, ham, coupling, projector, parts):
+    size = ham.shape[0]
+    part = size // parts
+    smem = pl.BlockSpec(memory_space=pltpu.SMEM)
+    vmem = pl.BlockSpec(memory_space=pltpu.VMEM)
+    return pl.pallas_call(
+        pack_kernel,
+        out_shape=(
+            jax.ShapeDtypeStruct((part // 2 + part + 8, size), F32),
+            jax.ShapeDtypeStruct((part, size), F32),
+        ),
+        in_specs=[smem, smem, vmem, vmem, vmem, vmem],
+        out_specs=(vmem, vmem),
+        scratch_shapes=[pltpu.VMEM((size // 2, size), F32)],
+        compiler_params=pltpu.CompilerParams(vmem_limit_bytes=VMEM_BYTES),
+        name="pack",
+    )(place, weight, level, ham, coupling, projector)
+
+
 def factor_kernel(
-    shift_ref, weight_ref, level_ref, ham_ref, coupling_ref, basis_ref, inverse_ref, link_ref,
-    diag_scr, matrix_scr, inverse_scr,
+    shift_ref, matrix_ref, basis_ref, inverse_ref, link_ref, diag_scr, coupling_ref,
+    matrix_scr, inverse_scr,
 ):
-    count = ham_ref.shape[0]
-    size = ham_ref.shape[1]
+    count, parts, height, size = matrix_ref.shape
+    part = size // parts
+    ham_part = part // 2
     middle = count // 2
     identity = eye_of(size)
     basis = split(basis_ref[...])
     potential = dot3(basis, basis, NT)
     for n in range(count):
-        ham = ham_ref[n]
+        packed = matrix_ref[n, :, :ham_part].reshape(size // 2, size)
+        coupling_ref[n] = matrix_ref[n, :, ham_part : ham_part + part].reshape(size, size)
+        diagonal = matrix_ref[n, 0, ham_part + part : ham_part + part + 1]
+        weight = matrix_ref[n, 0, ham_part + part + 1 : ham_part + part + 2, :1]
         diag_scr[n] = (
-            0.5 * (ham + ham.T)
-            + (2.0 + level_ref[n : n + 1, :] + shift_ref[0]) * identity
-            + weight_ref[n] * potential
+            unpack_symmetric(packed)
+            + (diagonal + shift_ref[0]) * identity
+            + weight * potential
         )
 
     def eliminate(invert):
@@ -151,37 +222,46 @@
         )
 
 
-def factorize(shift, weights, levels, ham, coupling, basis):
-    count, size = ham.shape[0], ham.shape[1]
+def factorize(shift, matrices, basis):
+    count, size = matrices.shape[0], matrices.shape[3]
     smem = pl.BlockSpec(memory_space=pltpu.SMEM)
     vmem = pl.BlockSpec(memory_space=pltpu.VMEM)
     half = jax.ShapeDtypeStruct((2, count, size, size), BF16)
     return pl.pallas_call(
         factor_kernel,
         out_shape=(half, half),
-        in_specs=[smem, smem, vmem, vmem, vmem, vmem],
+        in_specs=[smem, vmem, vmem],
         out_specs=(vmem, vmem),
         scratch_shapes=[
+            pltpu.VMEM((count, size, size), F32),
             pltpu.VMEM((count, size, size), F32),
             pltpu.VMEM((size, size), F32),
             pltpu.VMEM((size, size), F32),
         ],
         compiler_params=pltpu.CompilerParams(vmem_limit_bytes=VMEM_BYTES),
         name="factorize",
-    )(shift, weights, levels, ham, coupling, basis)
+    )(shift, matrices, basis)
 
 
 def solve_kernel(
-    place_ref, open_ref, weight_ref, inverse_ref, link_ref, source_ref, projector_ref,
-    target_ref, wave_ref, adjoint_ref, share_ref, gram_ref, own_scr, k_scr,
+    place_ref, open_ref, matrix_ref, inverse_ref, link_ref, projector_ref, target_ref,
+    *rest,
 ):
-    count = source_ref.shape[0]
-    channels, width = source_ref.shape[1:]
+    count = inverse_ref.shape[1]
+    source_refs, rest = rest[:count], rest[count:]
+    wave_ref, adjoint_ref, share_ref, gram_ref, own_scr, k_scr = rest
+    channels, width = source_refs[0].shape
     middle = count // 2
-    me, column = place_ref[0], place_ref[1]
+    me, column = place_ref[1], place_ref[2]
     inverses = [(inverse_ref[0, n], inverse_ref[1, n]) for n in range(count)]
     links = [(link_ref[0, n], link_ref[1, n]) if n != 0 else None for n in range(count)]
-    projectors = [split(projector_ref[n]) for n in range(count)]
+    projectors = [
+        split(projector_ref[n].reshape(channels, projector_ref.shape[3])) for n in range(count)
+    ]
+    weight_row = matrix_ref.shape[2] - 7
+    weights = [matrix_ref[n, 0, weight_row : weight_row + 1, :1] for n in range(count)]
+    for n in range(count):
+        own_scr[me ^ n] = source_refs[n][...]
 
     def solve(blocks):
         reduced = list(blocks)
@@ -200,7 +280,7 @@
             halves[n] = split(solved[n])
         return solved, halves
 
-    wave, wave_halves = solve([source_ref[n].T for n in range(count)])
+    wave, wave_halves = solve([own_scr[n].T for n in range(count)])
     k_total = dot3(wave_halves[0], projectors[0])
     for n in range(1, count):
         k_total = k_total + dot3(wave_halves[n], projectors[n])
@@ -222,13 +302,17 @@
     for n in range(count):
         own_scr[n] = adjoint[n]
     adjoint_ref[...] = own_scr[me]
-    weighted = jnp.concatenate([weight_ref[n] * wave[n] for n in range(count)], axis=1)
+    weighted = jnp.concatenate([weights[n] * wave[n] for n in range(count)], axis=1)
     gram = dot3(split(jnp.concatenate(adjoint, axis=1)), split(weighted), NT)
-    gram_ref[...] = gram + gram.T
-
-
-def solve_all(place, opened, weights, inverses, links, sources, projectors, target):
-    count, channels, width = sources.shape
+    gram = gram + gram.T
+    half = channels // 2
+    gram_ref[:half] = pack_symmetric(gram)
+    gram_ref[half:] = jnp.broadcast_to(diagonal_of(gram), (8, channels))
+
+
+def solve_all(place, opened, matrices, inverses, links, projectors, target, sources):
+    count = len(sources)
+    channels, width = sources[0].shape
     rows = target.shape[0]
     smem = pl.BlockSpec(memory_space=pltpu.SMEM)
     vmem = pl.BlockSpec(memory_space=pltpu.VMEM)
@@ -238,9 +322,9 @@
             jax.ShapeDtypeStruct((channels, width), F32),
             jax.ShapeDtypeStruct((channels, width), F32),
             jax.ShapeDtypeStruct((rows // count, width), F32),
-            jax.ShapeDtypeStruct((channels, channels), F32),
+            jax.ShapeDtypeStruct((channels // 2 + 8, channels), F32),
         ),
-        in_specs=[smem, smem, smem, vmem, vmem, vmem, vmem, vmem],
+        in_specs=[smem, smem] + [vmem] * (5 + count),
         out_specs=(vmem,) * 4,
         scratch_shapes=[
             pltpu.VMEM((count, channels, width), F32),
@@ -248,18 +332,47 @@
         ],
         compiler_params=pltpu.CompilerParams(vmem_limit_bytes=VMEM_BYTES),
         name="solve",
-    )(place, opened, weights, inverses, links, sources, projectors, target)
-
-
-def total_over(value, axis):
+    )(place, opened, matrices, inverses, links, projectors, target, *sources)
+
+
+def gradient_kernel(scale, own_ref, other_ref, basis_ref, out_ref):
+    size = basis_ref.shape[0]
+    total = own_ref[...] + other_ref[...]
+    gram = unpack_symmetric(total[: size // 2])
+    gram = gram + total[size // 2 : size // 2 + 1] * eye_of(size)
+    out_ref[...] = scale * dot3(split(gram), split(basis_ref[...]))
+
+
+def gradient(scale, own, other, basis):
+    vmem = pl.BlockSpec(memory_space=pltpu.VMEM)
+    return pl.pallas_call(
+        functools.partial(gradient_kernel, scale),
+        out_shape=jax.ShapeDtypeStruct(basis.shape, F32),
+        in_specs=[vmem, vmem, vmem],
+        out_specs=vmem,
+        compiler_params=pltpu.CompilerParams(vmem_limit_bytes=VMEM_BYTES),
+        name="gradient",
+    )(own, other, basis)
+
+
+def swap(value, axis, step):
     count = lax.axis_size(axis)
-    if count & (count - 1):
-        return lax.psum(value, axis)
-    step = 1
-    while step < count:
-        value = value + lax.ppermute(value, axis, [(i, i ^ step) for i in range(count)])
-        step = step * 2
-    return value
+    return lax.ppermute(value, axis, [(i, i ^ step) for i in range(count)])
+
+
+def gradient_total(gram, scale, basis):
+    steps = []
+    for axis in ("rhs", "energy"):
+        step = 1
+        while step < lax.axis_size(axis):
+            steps.append((axis, step))
+            step = step * 2
+    other = jnp.zeros_like(gram)
+    for index, (axis, step) in enumerate(steps):
+        if index:
+            gram = gram + other
+        other = swap(gram, axis, step)
+    return gradient(scale, gram, other, basis)
 
 
 def per_device(
@@ -274,27 +387,25 @@
     target,
     open_channels,
 ):
-    elements = lax.axis_size("elem")
-    size = ham_noise.shape[1]
-    extra = jnp.concatenate(
-        [channel_levels, jnp.broadcast_to(corr_weight[:, None], (7, size))], axis=0
-    )
-    matrices = jnp.concatenate([ham_noise[0], coupling_noise[0], extra], axis=0)
-    matrices = lax.all_gather(matrices, "elem")
-    source_all = lax.all_gather(sources[0, 0], "elem")
-    projector_all = lax.all_gather(projector[0], "elem")
-    ham = matrices[:, :size]
-    coupling = matrices[:, size : 2 * size]
-    levels = matrices[:, 2 * size]
-    weights = matrices[:, 2 * size + 1, 0]
-    inverses, links = factorize(energy_shift, weights, levels, ham, coupling, corr_basis)
-    place = jnp.stack([lax.axis_index("elem"), lax.axis_index("rhs")]).astype(jnp.int32)
+    elements, energies, halves = (lax.axis_size(axis) for axis in ("elem", "energy", "rhs"))
+    parts = energies * halves
+    element, half = lax.axis_index("elem"), lax.axis_index("rhs")
+    quarter = lax.axis_index("energy") * halves + half
+    place = jnp.stack([quarter, element, half]).astype(jnp.int32)
+    matrices, projector_part = pack(
+        place, corr_weight, channel_levels, ham_noise[0], coupling_noise[0], projector[0], parts
+    )
+    own = sources[0, 0]
+    matrices = lax.all_gather(matrices, ("elem", "energy", "rhs"))
+    projectors = lax.all_gather(projector_part, ("elem", "energy", "rhs"))
+    source_all = [own] + [swap(own, "elem", step) for step in range(1, elements)]
+    matrices = matrices.reshape((elements, parts) + matrices.shape[1:])
+    projectors = projectors.reshape((elements, parts) + projectors.shape[1:])
+    inverses, links = factorize(energy_shift, matrices, corr_basis)
     wave, adjoint, share, gram = solve_all(
-        place, open_channels, weights, inverses, links, source_all, projector_all, target[0]
-    )
-    gram = total_over(total_over(gram, "rhs"), "energy")
-    grad = jnp.dot(gram, corr_basis, precision=lax.Precision.HIGHEST)
-    basis_grad = grad * (-1.0 / (lax.axis_size("energy") * elements))
+        place, open_channels, matrices, inverses, links, projectors, target[0], source_all
+    )
+    basis_grad = gradient_total(gram, -1.0 / (energies * elements), corr_basis)
     return wave[None, None], adjoint[None, None], share[None], basis_grad
 
 

time: 117 us -> 119 us (1.017)
  Pallas kernels: 12.6 us -> 37.4 us
  blocking collectives: 22.6 us -> 0 us
  waiting for transfers between devices: 56 us -> 49 us
  starting transfers between devices: 1.62 us -> 6.77 us
  local copies, waits for them, and re-layouts: 4.59 us -> 9.36 us
  other arithmetic: 2.11 us -> 0.1 us
    pallas_call x1 -> x3, Pallas kernels: 7.73 us -> 32.5 us  [the longest x1 30.2 us: factorize(): pl.pallas_call(factor_kernel, out_shape=(half, half), in_specs=[smem, vme...]
    all_gather x1 -> x0, blocking collectives: 22.6 us -> none  [per_device(): source_all = lax.all_gather(sources[0, 0], 'elem')]
    unnamed x7 -> x26, local copies, waits for them, and re-layouts: 1.24 us -> 9.36 us
    ppermute x2 -> x5, starting transfers between devices: 1.54 us -> 6.69 us  [swap(): return lax.ppermute(value, axis, [(i, i ^ step) for i in range(count)])]
    all_gather x2, waiting for transfers between devices: 46.9 us -> 41.9 us  [the longest x1 36.1 us: per_device(): matrices = lax.all_gather(matrices, ('elem', 'energy', 'rhs'))]
    slice x3 -> x0, local copies, waits for them, and re-layouts: 3.27 us -> none  [the longest x1 1.68 us: per_device(): coupling = matrices[:, size:2 * size]]
    ppermute x2 -> x5, waiting for transfers between devices: 8.41 us -> 6.34 us  [swap(): return lax.ppermute(value, axis, [(i, i ^ step) for i in range(count)])]
    concatenate x1 -> x0, other arithmetic: 2 us -> none  [per_device(): matrices = jnp.concatenate([ham_noise[0], coupling_noise[0], extra], axis=0)]
  transfers between devices with their start and end apart: 4 -> 7, of which waited for: 4 -> 4; matrix products, arithmetic and copies ran while one was open for 3% -> 0% of each run, Pallas kernels for 7% -> 25%
where the time goes in v2:
time: 119 us
  waiting for transfers between devices  49 us (41%)
  Pallas kernels  37.4 us (31%)
  between operations  16 us (13%)
  local copies, waits for them, and re-layouts  9.36 us (8%)
  starting transfers between devices  6.77 us (6%)
    all_gather x1, waiting for transfers between devices, per_device(): matrices = lax.all_gather(matrices, ('elem', 'energy', 'rhs'))  36.1 us
    pallas_call x1, Pallas kernels, factorize(): pl.pallas_call(factor_kernel, out_shape=(half, half), in_specs=[smem, vme...  30.2 us
    unnamed x26, local copies, waits for them, and re-layouts  9.36 us
    ppermute x5, starting transfers between devices, swap(): return lax.ppermute(value, axis, [(i, i ^ step) for i in range(count)])  6.69 us
    ppermute x5, waiting for transfers between devices, swap(): return lax.ppermute(value, axis, [(i, i ^ step) for i in range(count)])  6.34 us
    all_gather x1, waiting for transfers between devices, per_device(): projectors = lax.all_gather(projector_part, ('elem', 'energy', 'rhs'))  5.82 us
    pallas_call x1, Pallas kernels, solve_all(): pl.pallas_call(solve_kernel, out_shape=(jax.ShapeDtypeStruct((channels, w...  4.91 us
  transfers between devices with their start and end apart: 7, of which 4 were waited for; matrix products, arithmetic and copies ran while one was open for 0% of the time, Pallas kernels for 25%

profile of v2, /device:TPU:0, one launch (start us, length us, event | category | flops | bytes accessed | tf_op | source)
XLA Modules:
  0.0 118.7 jit_solution(3197548883792838862)
XLA Ops:
  7.9 0.1 pad_add_fusion.place_ref
  7.9 0.9 copy-done.7
  8.9 0.9 copy-done.8
  9.8 0.9 copy-done.9
  10.8 0.7 copy-done.12
  11.5 1.3 %pack.1 = (f32[104,256]{1,0:T(8,128)}, f32[64,256]{1,0:T(8,128)}) custom-call(s32[3]{0:T(128)S(1)} %pad_add_fusion.place_ref, f32[1]{0:T(128)S(6)} %copy.14.weight_ref, f32[1,256]{1,0:T(1,128)S(1)} %copy-done.12, f32[256,256]{1,0:T(8,128)S(1)} %bitcast.16, f32[256,256]{1,0:T(8,128)S(1)} %bitcast.17, f32[256,256]{1,0:T(8,128)S(1)} %bitcast.18), custom_call_target="tpu_custom_call" | custom-call | tf_op jit(solution)/shard_map/pack/pallas_call | solution.py:138
  12.8 0.0 all-gather.7.cloned.1.call-start
  12.9 0.7 all-gather.7.cloned.1.call-update
  13.6 5.1 %collective-permute-start.2 = (f32[256,128]{1,0:T(8,128)}, f32[256,128]{1,0:T(8,128)S(1)}, u32[]{:S(2)}, u32[]{:S(2)}) collective-permute-start(f32[256,128]{1,0:T(8,128)} %bitcast.20), channel_id=1, source_target_pairs={{0,12},{4,8},{8,4},{12,0},{1,13},{5,9},{9,5},{13,1},{2,14},{6,10},... | collective-permute-start | bytes 393224 | tf_op jit(solution)/shard_map/ppermute | solution.py:360
  18.7 0.6 collective-permute-start
  20.7 36.1 %all-gather.5.cloned.1.call-done = f32[1664,256]{1,0:T(8,128)} async-done(((f32[104,256]{1,0:T(8,128)}), f32[1664,256]{1,0:T(8,128)}) %all-gather.5.cloned.1.call-update) | async-done | bytes 1703952 | tf_op jit(solution)/shard_map/all_gather | solution.py:399
  56.8 1.5 %copy-done = f32[1664,256]{1,0:T(8,128)S(1)} copy-done((f32[1664,256]{1,0:T(8,128)S(1)}, f32[1664,256]{1,0:T(8,128)}, u32[]{:S(2)}) %copy-start) | copy-done | bytes 1703960
  58.2 0.9 copy-done.2
  59.2 30.2 %factorize.1 = (bf16[2,4,256,256]{3,2,1,0:T(8,128)(2,1)S(1)}, bf16[2,4,256,256]{3,2,1,0:T(8,128)(2,1)S(1)}) custom-call(f32[1]{0:T(128)S(6)} %copy.15.shift_ref, f32[4,4,104,256]{3,2,1,0:T(8,128)S(1)} %bitcast.13, f32[256,256]{1,0:T(8,128)S(1)} %copy-done.2), custom_call_target="tpu_custom_call" | custom-call | tf_op jit(solution)/shard_map/factorize/pallas_call | solution.py:230
  89.3 1.0 copy-done.5
  90.3 5.8 %all-gather.7.cloned.1.call-done = f32[1024,256]{1,0:T(8,128)} async-done(((f32[64,256]{1,0:T(8,128)}), f32[1024,256]{1,0:T(8,128)}) %all-gather.7.cloned.1.call-update) | async-done | bytes 1048592 | tf_op jit(solution)/shard_map/all_gather | solution.py:400
  96.2 1.2 %copy-done.4 = f32[1024,256]{1,0:T(8,128)S(1)} copy-done((f32[1024,256]{1,0:T(8,128)S(1)}, f32[1024,256]{1,0:T(8,128)}, u32[]{:S(2)}) %copy-start.4) | copy-done | bytes 1048600
  97.4 1.2 %copy-done.6 = bf16[2,4,256,256]{3,2,1,0:T(8,128)(2,1)S(1)} copy-done((bf16[2,4,256,256]{3,2,1,0:T(8,128)(2,1)S(1)}, bf16[2,4,256,256]{3,2,1,0:T(8,128)(2,1)}, u32[]{:S(2)}) %copy-start.6) | copy-done | bytes 1048600
  98.6 4.9 %solve.1 = (f32[256,128]{1,0:T(8,128)}, f32[256,128]{1,0:T(8,128)}, f32[64,128]{1,0:T(8,128)}, f32[136,256]{1,0:T(8,128)S(1)}) custom-call(s32[3]{0:T(128)S(1)} %pad_add_fusion.place_ref, s32[1]{0:T(128)S(6)} %copy.16.open_ref, f32[4,4,104,256]{3,2,1,0:T(8,128)S(1)} %bitcast.14, bf16[2,4,256,256]{3,2,1,0:T(8,128)(2,1)S(1)} %get-tuple-element.13.inverse_ref, ...), custom_call_target="tpu_custom_call" | custom-call | tf_op jit(solution)/shard_map/solve/pallas_call | solution.py:319
  103.5 0.3 collective-permute-start.3
  103.8 1.1 collective-permute-done.3
  104.9 0.7 collective-permute-start.4
  105.6 5.2 %collective-permute-done.4.other_ref = f32[136,256]{1,0:T(8,128)S(1)} collective-permute-done((f32[136,256]{1,0:T(8,128)S(1)}, f32[136,256]{1,0:T(8,128)S(1)}, u32[]{:S(2)}, u32[]{:S(2)}) %collective-permute-start.4) | collective-permute-done | bytes 139296 | tf_op jit(solution)/shard_map/ppermute | solution.py:360
  110.8 1.0 gradient.1
  (24 shorter events, 0.1 us)
Async XLA Ops:
  7.2 49.6 %all-gather.5.cloned.1.call-start = ((), (), s32[]{:S(2)}) async-start(), calls=%async_computation | async-start | bytes 1810432 | tf_op jit(solution)/shard_map/all_gather | solution.py:399
  7.9 1.0 copy-start.7
  8.9 0.9 copy-start.8
  9.8 0.9 copy-start.9
  10.8 0.7 copy-start.12
  11.5 84.7 %copy-start.10 = (f32[1,256,128]{2,1,0:T(8,128)S(1)}, f32[1,256,128]{2,1,0:T(8,128)}, u32[]{:S(2)}) copy-start(f32[1,256,128]{2,1,0:T(8,128)} %param.18) | copy-start | bytes 393220
  11.5 84.7 %copy-start.11 = (f32[1,1,256,128]{3,2,1,0:T(8,128)S(1)}, f32[1,1,256,128]{3,2,1,0:T(8,128)}, u32[]{:S(2)}) copy-start(f32[1,1,256,128]{3,2,1,0:T(8,128)} %param.17) | copy-start | bytes 393220
  12.8 83.3 %all-gather.7.cloned.1.call-start = ((), (), s32[]{:S(2)}) async-start(), calls=%async_computation.1 | async-start | bytes 1114112 | tf_op jit(solution)/shard_map/all_gather | solution.py:400
  13.6 76.7 %collective-permute-start.2 = (f32[256,128]{1,0:T(8,128)}, f32[256,128]{1,0:T(8,128)S(1)}, u32[]{:S(2)}, u32[]{:S(2)}) collective-permute-start(f32[256,128]{1,0:T(8,128)} %bitcast.20), channel_id=1, source_target_pairs={{0,12},{4,8},{8,4},{12,0},{1,13},{5,9},{9,5},{13,1},{2,14},{6,10},... | collective-permute-start | bytes 393224 | tf_op jit(solution)/shard_map/ppermute | solution.py:360
  18.7 71.6 %collective-permute-start.1 = (f32[256,128]{1,0:T(8,128)}, f32[256,128]{1,0:T(8,128)S(1)}, u32[]{:S(2)}, u32[]{:S(2)}) collective-permute-start(f32[256,128]{1,0:T(8,128)} %bitcast.21), channel_id=1, source_target_pairs={{0,8},{4,12},{8,0},{12,4},{1,9},{5,13},{9,1},{13,5},{2,10},{6,14},... | collective-permute-start | bytes 393224 | tf_op jit(solution)/shard_map/ppermute | solution.py:360
  18.7 71.6 %collective-permute-start = (f32[256,128]{1,0:T(8,128)}, f32[256,128]{1,0:T(8,128)S(1)}, u32[]{:S(2)}, u32[]{:S(2)}) collective-permute-start(f32[256,128]{1,0:T(8,128)} %bitcast.22), channel_id=1, source_target_pairs={{0,4},{4,0},{8,12},{12,8},{1,5},{5,1},{9,13},{13,9},{2,6},{6,2},{1... | collective-permute-start | bytes 393224 | tf_op jit(solution)/shard_map/ppermute | solution.py:360
  56.8 1.5 %copy-start = (f32[1664,256]{1,0:T(8,128)S(1)}, f32[1664,256]{1,0:T(8,128)}, u32[]{:S(2)}) copy-start(f32[1664,256]{1,0:T(8,128)} %all-gather.5.cloned.1.call-done) | copy-start | bytes 5111812
  58.2 0.9 copy-start.2
  59.2 37.0 %copy-start.1 = (f32[1664,256]{1,0:T(8,128)S(1)}, f32[1664,256]{1,0:T(8,128)}, u32[]{:S(2)}) copy-start(f32[1664,256]{1,0:T(8,128)} %all-gather.5.cloned.1.call-done) | copy-start | bytes 5111812
  89.3 1.0 copy-start.5
  96.2 1.2 %copy-start.4 = (f32[1024,256]{1,0:T(8,128)S(1)}, f32[1024,256]{1,0:T(8,128)}, u32[]{:S(2)}) copy-start(f32[1024,256]{1,0:T(8,128)} %all-gather.7.cloned.1.call-done) | copy-start | bytes 3145732
  97.4 1.2 %copy-start.6 = (bf16[2,4,256,256]{3,2,1,0:T(8,128)(2,1)S(1)}, bf16[2,4,256,256]{3,2,1,0:T(8,128)(2,1)}, u32[]{:S(2)}) copy-start(bf16[2,4,256,256]{3,2,1,0:T(8,128)(2,1)} %copy-done.5) | copy-start | bytes 3145732
  98.6 12.2 %copy-start.3 = (f32[256,256]{1,0:T(8,128)S(1)}, f32[256,256]{1,0:T(8,128)}, u32[]{:S(2)}) copy-start(f32[256,256]{1,0:T(8,128)} %basis_ref.3) | copy-start | bytes 786436
  103.5 1.4 %collective-permute-start.3 = (f32[136,256]{1,0:T(8,128)S(1)}, f32[136,256]{1,0:T(8,128)S(1)}, u32[]{:S(2)}, u32[]{:S(2)}) collective-permute-start(f32[136,256]{1,0:T(8,128)S(1)} %get-tuple-element.19), channel_id=1, source_target_pairs={{0,1},{1,0},{2,3},{3,2},{4,5},{5,4},{6,7},{7,6},{8,9},{9,8},{10,11... | collective-permute-start | bytes 417800 | tf_op jit(solution)/shard_map/ppermute | solution.py:360
  104.9 5.9 %collective-permute-start.4 = (f32[136,256]{1,0:T(8,128)S(1)}, f32[136,256]{1,0:T(8,128)S(1)}, u32[]{:S(2)}, u32[]{:S(2)}) collective-permute-start(f32[136,256]{1,0:T(8,128)S(1)} %add.7.own_ref), channel_id=1, source_target_pairs={{0,2},{2,0},{1,3},{3,1},{4,6},{6,4},{5,7},{7,5},{8,10},{10,8},{9,1... | collective-permute-start | bytes 417800 | tf_op jit(solution)/shard_map/ppermute | solution.py:360
Sparse Core Ops, SparseCore 0:
  13.0 43.7 all-gather.4
  59.5 36.5 all-gather.6
